TPU v7x, 32 devices: a whole 2x2x4 slice. The times are simulated.
32 devices in a mesh: fsdp: 8 (over z, y), seq: 4 (over x, core).
Axes of the slice: x: 2, y: 2, z: 4, core: 2. Of those that a mesh axis runs over, the one named last changes fastest.
Arguments:
- text_embeds: bfloat16 [2240, 4096], P('fsdp'), may hold values from -8 to 8
- vision_tokens: bfloat16 [1024, 4096], P('fsdp', 'seq'), may hold values from -6 to 6
- vision_request: int32 [1024, 1], P('fsdp'), may hold values from 0 to 7; in each aligned block of 128 rows (0 to 127, 128 to 255, ...) at most 32 rows name the same one
- image_start: int32 [8], P('fsdp'), may hold values from 1 to 16
- lengths: int32 [8], P('fsdp'), may hold values from 273 to 280
- attn_gain: float32 [4096], replicated, may hold values from 0.5 to 1.5
- w_query: bfloat16 [4096, 2048], P('fsdp', 'seq'), may hold values from -1 to 1
- w_key: bfloat16 [4096, 2048], P('fsdp', 'seq'), may hold values from -1 to 1
- w_value: bfloat16 [4096, 2048], P('fsdp', 'seq'), may hold values from -0.09375 to 0.09375
- w_out: bfloat16 [2048, 4096], P(None, 'fsdp'), may hold values from -0.125 to 0.125
- final_gain: float32 [4096], replicated, may hold values from 0.25 to 1.75
- lm_head: bfloat16 [4096, 32000], P(None, 'fsdp'), may hold values from -0.25 to 0.25
Outputs:
- state_rms: float32 [8], P('seq')
- max_logit: float32 [8], P('seq')
Inputs may be any that keep to these rules, and one draw needn't show every extreme that they name: `vision_request`: within the 128 vision tokens of one index of fsdp no request is named more than 32 times, a bound that some block reaches; every request is named by some vision token. `lengths`: each request's image tokens end before its last token.
All inputs are finite; a program needn't handle non-finite values.
Results may differ from a plain program's by a relative error of at most 0.0024.
Values may be sent and summed in bfloat16 or wider, within the bound.
A program may use at most 128 MiB of HBM per device.

v0:
```python
import functools
import math

import jax
import jax.numpy as jnp
from jax import lax
from jax.experimental import pallas as pl
from jax.experimental.pallas import tpu as pltpu
from jax.sharding import PartitionSpec as P

HD = 128


norm_epsilon = 1e-05


def row_norm(rows, gain):
    widened = rows.astype(jnp.float32)
    return (
        widened
        * lax.rsqrt(jnp.mean(widened * widened, axis=1, keepdims=True) + norm_epsilon)
        * gain
    ).astype(jnp.bfloat16)


def pack_slots(tokens, destination, slot_index, groups, capacity):
    return (
        jnp.zeros((groups, capacity, tokens.shape[1]), jnp.bfloat16)
        .at[destination, slot_index]
        .set(tokens)
    )


def local(
    text_embeds,
    vision_tokens,
    vision_request,
    image_start,
    lengths,
    attn_gain,
    w_query,
    w_key,
    w_value,
    w_out,
    final_gain,
    lm_head,
):
    groups = lax.axis_size("fsdp")
    seq_count = lax.axis_size("seq")
    group_index = lax.axis_index("fsdp")
    seq_index = lax.axis_index("seq")
    seq_len = text_embeds.shape[0]
    width = text_embeds.shape[1]
    columns = w_key.shape[1]
    heads_local = columns // HD
    dpiece = width // groups
    fpiece = width // seq_count
    quarter = groups // seq_count
    capacity = max(2, 2 * vision_tokens.shape[0] // groups)
    last_index = lengths[0] - 1
    destination = vision_request[:, 0]
    onehot = (destination[:, None] == jnp.arange(groups, dtype=jnp.int32)[None, :]).astype(
        jnp.int32
    )
    slot_index = jnp.sum((jnp.cumsum(onehot, axis=0) - onehot) * onehot, axis=1)
    counts = jnp.sum(onehot, axis=0)
    outbox = pack_slots(vision_tokens, destination, slot_index, groups, capacity)
    final_text = lax.dynamic_slice_in_dim(text_embeds, last_index, 1, 0)
    last_row = row_norm(final_text, attn_gain)
    last_pieces = jnp.stack(
        [last_row.reshape(groups, dpiece), final_text.reshape(groups, dpiece)], axis=1
    )
    last_parts = lax.all_to_all(last_pieces, "fsdp", split_axis=0, concat_axis=0, tiled=True)
    received = lax.all_to_all(outbox, "fsdp", split_axis=0, concat_axis=0, tiled=True)
    arrived = lax.all_to_all(counts[:, None], "fsdp", split_axis=0, concat_axis=0, tiled=True)
    query = lax.psum(
        jnp.dot(last_parts[:, 0], w_query, preferred_element_type=jnp.float32), "fsdp"
    ).astype(jnp.bfloat16)
    gain_part = lax.dynamic_slice_in_dim(attn_gain, group_index * dpiece, dpiece, 0)
    probe_part = (
        jnp.einsum(
            "rhc,dhc->rhd",
            query.reshape(groups, heads_local, HD),
            w_key.reshape(dpiece, heads_local, HD),
            preferred_element_type=jnp.float32,
        )
        * gain_part
    ).astype(jnp.bfloat16)
    probe = lax.all_to_all(probe_part, "fsdp", split_axis=0, concat_axis=0, tiled=True)
    probe = probe.transpose(1, 0, 2).reshape(heads_local, width)
    probe = lax.all_to_all(probe, "seq", split_axis=1, concat_axis=0, tiled=True)
    occupied = (
        (jnp.arange(capacity, dtype=jnp.int32)[None, :] < arrived).astype(jnp.int32).reshape(-1)
    )
    ranking = jnp.cumsum(occupied) - occupied
    positions = jnp.where(occupied > 0, image_start[0] + ranking, seq_len)
    text_piece = lax.dynamic_slice_in_dim(text_embeds, seq_index * fpiece, fpiece, 1)
    states = text_piece.at[positions].set(received.reshape(-1, fpiece), mode="drop")
    widened = states.astype(jnp.float32)
    squares = jnp.sum(widened * widened, axis=1)
    partial_scores = jnp.einsum("hd,jd->hj", probe, states, preferred_element_type=jnp.float32)
    summed = lax.psum(jnp.concatenate([partial_scores, squares[None, :]], axis=0), "seq")
    inverse = lax.rsqrt(summed[-1:] / width + norm_epsilon)
    scores = summed[:-1] * inverse / math.sqrt(HD)
    live_keys = jnp.arange(seq_len, dtype=jnp.int32) < lengths[0]
    scores = jnp.where(live_keys[None, :], scores, -jnp.inf)
    peak = jnp.max(scores, axis=1, keepdims=True)
    shifted = jnp.exp(scores - peak)
    weights = shifted / jnp.sum(shifted, axis=1, keepdims=True)
    mixed = jnp.dot(
        (weights * inverse).astype(jnp.bfloat16), states, preferred_element_type=jnp.float32
    )
    mixed_gain = lax.dynamic_slice_in_dim(attn_gain, seq_index * fpiece, fpiece, 0)
    mixed = (mixed * mixed_gain).astype(jnp.bfloat16)
    mixed = lax.all_to_all(mixed, "seq", split_axis=0, concat_axis=1, tiled=True)
    mixed = mixed.reshape(heads_local, groups, dpiece).transpose(1, 0, 2)
    mixed = lax.all_to_all(mixed, "fsdp", split_axis=0, concat_axis=0, tiled=True)
    attended = lax.psum(
        jnp.einsum(
            "rhd,dhc->rhc",
            mixed,
            w_value.reshape(dpiece, heads_local, HD),
            preferred_element_type=jnp.float32,
        ).reshape(groups, columns),
        "fsdp",
    ).astype(jnp.bfloat16)
    out_rows = lax.dynamic_slice_in_dim(w_out, seq_index * columns, columns, 0)
    projected = lax.psum(jnp.dot(attended, out_rows, preferred_element_type=jnp.float32), "seq")
    residual_out = last_parts[:, 1].astype(jnp.float32) + projected
    residual_out = lax.dynamic_slice_in_dim(residual_out, seq_index * quarter, quarter, 0)
    final_part = lax.dynamic_slice_in_dim(final_gain, group_index * dpiece, dpiece, 0)
    scaled_out = (residual_out * final_part[None, :]).astype(jnp.bfloat16)
    square_part = jnp.sum(residual_out * residual_out, axis=1)
    full_scaled = lax.all_gather(scaled_out, "fsdp", axis=1, tiled=True)
    mean_square = lax.psum(square_part, "fsdp") / width
    logits = jnp.dot(full_scaled, lm_head, preferred_element_type=jnp.float32)
    local_max = jnp.max(logits, axis=1) * lax.rsqrt(mean_square + norm_epsilon)
    max_logit = lax.pmax(local_max, "fsdp")
    return (jnp.sqrt(mean_square), max_logit)


MESH = pl.DeviceIdType.MESH
F32 = jnp.float32
BF16 = jnp.bfloat16


def dot(a, b):
    return jnp.dot(a, b, preferred_element_type=F32)


def dot_rows(a, b):
    return lax.dot_general(a, b, (((1,), (1,)), ((), ())), preferred_element_type=F32)


def iota(shape, axis):
    return lax.broadcasted_iota(jnp.int32, shape, axis)


def folded(rows):
    half = rows.shape[1] // 2
    return jnp.concatenate([rows[:, :half], rows[:, half:]], axis=0).astype(BF16)


def unfolded(rows):
    half = rows.shape[0] // 2
    return jnp.concatenate([rows[:half], rows[half:]], axis=1)


def wrap(index, size):
    return jnp.where(index >= size, index - size, index)


def fused_kernel(
    groups,
    seq_count,
    capacity,
    request,
    start,
    lengths,
    attn_gain,
    final_gain,
    text_hbm,
    vision_hbm,
    wq_hbm,
    wk_hbm,
    wv_hbm,
    wo_hbm,
    lm_hbm,
    rms_out,
    max_out,
    text,
    vision,
    wq,
    wk,
    wv,
    wo,
    lm,
    states,
    heads_in,
    stage,
    last_send,
    last_recv,
    box_send,
    box_recv,
    query_send,
    query_recv,
    key_send,
    key_recv,
    score_recv,
    mix_send,
    mix_recv,
    att_send,
    att_recv,
    out_recv,
    scaled_send,
    scaled_recv,
    peak_send,
    peak_row,
    peak_recv,
    local_sem,
    send_sem,
    recv_sem,
):
    f = lax.axis_index("fsdp")
    s = lax.axis_index("seq")
    devices = groups * seq_count
    seq_len, width = text.shape
    rows_per = width // groups
    piece = width // seq_count
    owners = groups // seq_count
    columns = wq.shape[1]
    local_heads = columns // HD
    heads = local_heads * seq_count
    vtok = vision.shape[0]
    half = rows_per // 2
    chunks = rows_per // 128

    barrier = pltpu.get_barrier_semaphore()
    me = f * seq_count + s

    others = []
    for k in range(groups):
        for j in range(seq_count):
            if k or j:
                others.append((wrap(f + k, groups), wrap(s + j, seq_count)))
    for other in others:
        pl.semaphore_signal(barrier, inc=1, device_id=other, device_id_type=MESH)

    def fetch(index, source, target):
        copy = pltpu.make_async_copy(source, target, local_sem.at[index])
        copy.start()
        return copy

    get_text = fetch(0, text_hbm, text)
    get_vision = fetch(1, vision_hbm, vision)
    get_wq = fetch(2, wq_hbm, wq)
    get_wk = fetch(3, wk_hbm, wk)

    sent = []

    def copy_of(phase, slot, from_slot, source, target, to_f, to_s):
        return pltpu.make_async_remote_copy(
            src_ref=source,
            dst_ref=target,
            send_sem=send_sem.at[phase, slot],
            recv_sem=recv_sem.at[phase, from_slot],
            device_id=(to_f, to_s),
            device_id_type=MESH,
        )

    def push(*what):
        copy = copy_of(*what)
        copy.start()
        sent.append(copy)

    def arrive(phase, slot, target):
        copy_of(phase, 0, slot, target, target, f, s).wait_recv()

    def across_groups(phase, source, target):
        for k in range(1, groups):
            t = wrap(f + k, groups)
            push(phase, k, f, source(t), target(f), t, s)

    def from_groups(phase, target):
        for k in range(1, groups):
            o = wrap(f + groups - k, groups)
            arrive(phase, o, target(o))

    def across_seq(phase, source, target):
        for k in range(1, seq_count):
            t = wrap(s + k, seq_count)
            push(phase, k, s, source(t), target(s), f, t)

    def from_seq(phase, target):
        for k in range(1, seq_count):
            o = wrap(s + seq_count - k, seq_count)
            arrive(phase, o, target(o))

    length = lengths[0]
    tail = (seq_len - 8) // 16 * 16
    get_text.wait()
    get_wv = fetch(4, wv_hbm, wv)
    get_wo = fetch(5, wo_hbm.at[pl.ds(pl.multiple_of(s * columns, columns), columns)], wo)
    words = lm.shape[0]
    vocab = lm_hbm.shape[0]
    final_seq = s == seq_count - 1
    final_words = vocab - (seq_count - 1) * words
    get_lm = pltpu.make_async_copy(
        lm_hbm.at[pl.ds(pl.multiple_of(s * words, words), words)], lm, local_sem.at[6]
    )
    get_lm_final = pltpu.make_async_copy(
        lm_hbm.at[vocab - final_words :], lm.at[:final_words], local_sem.at[6]
    )

    @pl.when(jnp.logical_not(final_seq))
    def _():
        get_lm.start()

    @pl.when(final_seq)
    def _():
        get_lm_final.start()
        if final_words < words:
            lm[final_words:, :] = jnp.zeros((words - final_words, width), BF16)

    tail_rows = text[tail:, :].astype(F32)
    here = iota((seq_len - tail, 1), 0) == length - 1 - tail
    last = jnp.sum(jnp.where(here, tail_rows, 0.0), axis=0, keepdims=True)
    scale = lax.rsqrt(jnp.mean(last * last, axis=1, keepdims=True) + norm_epsilon)
    normed = (last * scale * attn_gain[...]).astype(BF16).astype(F32)
    named = request[...]
    member = jnp.where(iota((groups, vtok), 0) == named, 1.0, 0.0)
    counts = jnp.broadcast_to(jnp.sum(member, axis=1, keepdims=True), (groups, rows_per))
    for g in range(groups):
        span = slice(g * rows_per, (g + 1) * rows_per)
        last_send[g, 0:1, :] = normed[:, span]
        last_send[g, 1:2, :] = last[:, span]
        last_send[g, 2:3, :] = counts[g : g + 1, :]
    last_recv[f] = last_send[f]

    earlier = jnp.where(iota((vtok, vtok), 0) < iota((vtok, vtok), 1), 1.0, 0.0)
    before = dot(member.astype(BF16), earlier.astype(BF16))
    rank = jnp.sum(before * member, axis=0, keepdims=True)
    slot = named.astype(F32) * capacity + rank
    slots = groups * capacity
    pick = jnp.where(iota((slots, vtok), 0).astype(F32) == slot, 1.0, 0.0).astype(BF16)
    get_vision.wait()
    box_send[...] = dot(pick, vision[...]).astype(BF16).reshape(groups, capacity, piece)
    box_recv[f] = box_send[f]
    pl.semaphore_wait(barrier, devices - 1)
    across_groups(0, lambda t: last_send.at[t], lambda me_f: last_recv.at[me_f])

    across_groups(2, lambda t: box_send.at[t], lambda me_f: box_recv.at[me_f])

    from_groups(0, lambda o: last_recv.at[o])
    get_wq.wait()
    query_part = dot(last_recv[:, 0, :].astype(BF16), wq[...])
    query_send[...] = folded(query_part)
    query_recv[f] = query_send[...]
    across_groups(3, lambda t: query_send, lambda me_f: query_recv.at[me_f])
    get_wk.wait()
    from_groups(3, lambda o: query_recv.at[o])
    query = unfolded(jnp.sum(query_recv[...].astype(F32), axis=0)).astype(BF16)

    gain_rows = attn_gain[:, pl.ds(pl.multiple_of(f * rows_per, rows_per), rows_per)]
    for h in range(local_heads):
        span = slice(h * HD, (h + 1) * HD)
        probe = dot_rows(query[:, span], wk[:, span]) * gain_rows
        for c in range(chunks):
            stage[:, c * local_heads + h, :] = probe[:, c * 128 : (c + 1) * 128]
    key_send[...] = stage[...].astype(BF16)
    home = lax.div(f, owners)
    inner = lax.rem(f, owners)
    at_home = home == s
    own_key = copy_of(4, 0, inner * seq_count + s, key_send.at[f], key_recv.at[inner, s], f, home)

    @pl.when(at_home)
    def _():
        key_recv[inner, s] = key_send[f]

    @pl.when(jnp.logical_not(at_home))
    def _():
        own_key.start()

    for k in range(1, groups):
        t = wrap(f + k, groups)
        push(4, k, inner * seq_count + s, key_send.at[t], key_recv.at[inner, s], t, home)

    tally = last_recv[:, 2, :128]
    tallies = jnp.concatenate([tally] * (slots // 128), axis=1)
    source_of = iota((groups, slots), 0)
    owner = lax.div(iota((groups, slots), 1), capacity)
    arrived = jnp.sum(jnp.where(source_of == owner, tallies, 0.0), axis=0, keepdims=True)
    offset = jnp.sum(jnp.where(source_of < owner, tallies, 0.0), axis=0, keepdims=True)
    within = lax.rem(iota((1, slots), 1), capacity).astype(F32)
    first = start[0].astype(F32)
    position = jnp.where(within < arrived, first + offset + within, -1.0)
    place = jnp.where(iota((seq_len, slots), 0).astype(F32) == position, 1.0, 0.0).astype(BF16)
    total = jnp.sum(tally[:, :1], axis=0, keepdims=True)
    row = iota((seq_len, 1), 0).astype(F32)
    taken = jnp.logical_and(row >= first, row < first + total)
    from_groups(2, lambda o: box_recv.at[o])
    step = min(256, piece)
    squares = jnp.zeros((seq_len, 1), F32)
    for c in range(piece // step):
        span = slice(c * step, (c + 1) * step)
        placed = dot(place, box_recv[:, :, span].reshape(slots, step))
        at = pl.multiple_of(s * piece + c * step, step)
        value = jnp.where(taken, placed, text[:, pl.ds(at, step)].astype(F32))
        states[:, span] = value.astype(BF16)
        squares = squares + jnp.sum(value * value, axis=1, keepdims=True)

    for b in range(owners):
        for k in range(seq_count):
            o = wrap(s + k, seq_count)
            if k:
                arrive(4, b * seq_count + o, key_recv.at[b, o])
            else:

                @pl.when(jnp.logical_not(f == s * owners + b))
                def _(o=o, b=b):
                    arrive(4, b * seq_count + o, key_recv.at[b, o])

    for o in range(seq_count):
        for b in range(owners):
            block = key_recv[b, o].astype(F32)
            for c in range(chunks):
                at = b * rows_per + c * 128
                heads_in[o * local_heads : (o + 1) * local_heads, at : at + 128] = block[
                    c * local_heads : (c + 1) * local_heads
                ]
    heads_in[heads:, :] = jnp.zeros((8, piece), F32)
    part = dot_rows(states[...], heads_in[...].astype(BF16))
    part = jnp.where(iota((1, heads + 8), 1) == heads, squares, part)
    score_recv[s] = part.T
    across_seq(5, lambda t: score_recv.at[s], lambda me_s: score_recv.at[me_s])
    from_seq(5, lambda o: score_recv.at[o])
    summed = jnp.sum(score_recv[...], axis=0)
    inverse = lax.rsqrt(summed[heads : heads + 1] / width + norm_epsilon)
    live = iota((1, seq_len), 1) < length
    scores = jnp.where(live, summed[:heads] * inverse / math.sqrt(HD), -jnp.inf)
    shifted = jnp.exp(scores - jnp.max(scores, axis=1, keepdims=True))
    weights = shifted / jnp.sum(shifted, axis=1, keepdims=True)
    mixed = dot((weights * inverse).astype(BF16), states[...])
    mixed = mixed * attn_gain[:, pl.ds(pl.multiple_of(s * piece, piece), piece)]

    for o in range(seq_count):
        for b in range(owners):
            rows = mixed[o * local_heads : (o + 1) * local_heads]
            starts = [b * rows_per + c * 128 for c in range(chunks)]
            mix_send[b, o] = jnp.concatenate(
                [rows[:, at : at + 128] for at in starts], axis=0
            ).astype(BF16)
    own_mix = []
    for b in range(owners):
        t = s * owners + b
        copy = copy_of(6, b * seq_count, f, mix_send.at[b, s], mix_recv.at[f], t, s)
        own_mix.append((t, copy))

        @pl.when(f == t)
        def _(b=b):
            mix_recv[f] = mix_send[b, s]

        @pl.when(jnp.logical_not(f == t))
        def _(copy=copy):
            copy.start()

        for k in range(1, seq_count):
            o = wrap(s + k, seq_count)
            push(6, b * seq_count + k, f, mix_send.at[b, o], mix_recv.at[f], t, o)
    get_wv.wait()
    from_groups(6, lambda o: mix_recv.at[o])

    @pl.when(jnp.logical_not(at_home))
    def _():
        arrive(6, f, mix_recv.at[f])

    stage[...] = mix_recv[...].astype(F32)
    att_part = []
    for h in range(local_heads):
        rows = [stage[:, c * local_heads + h, :] for c in range(chunks)]
        rows = jnp.concatenate(rows, axis=1).astype(BF16)
        att_part.append(dot(rows, wv[:, h * HD : (h + 1) * HD]))
    att_send[...] = folded(jnp.concatenate(att_part, axis=1))
    att_recv[f] = att_send[...]
    across_groups(7, lambda t: att_send, lambda me_f: att_recv.at[me_f])
    get_wo.wait()
    from_groups(7, lambda o: att_recv.at[o])
    attended = unfolded(jnp.sum(att_recv[...].astype(F32), axis=0)).astype(BF16)

    out_recv[s] = dot(attended, wo[...])
    across_seq(8, lambda t: out_recv.at[s], lambda me_s: out_recv.at[me_s])
    from_seq(8, lambda o: out_recv.at[o])
    residual = last_recv[:, 1, :] + jnp.sum(out_recv[...], axis=0)
    square_part = jnp.sum(residual * residual, axis=1, keepdims=True)
    final_rows = final_gain[:, pl.ds(pl.multiple_of(f * rows_per, rows_per), rows_per)]
    scaled = residual * final_rows
    scaled_send[...] = folded(scaled)

    scaled_recv[f] = scaled_send[...]
    across_groups(9, lambda t: scaled_send, lambda me_f: scaled_recv.at[me_f])

    @pl.when(jnp.logical_not(final_seq))
    def _():
        get_lm.wait()

    @pl.when(final_seq)
    def _():
        get_lm_final.wait()

    logits = jnp.zeros((groups, words), F32)
    for k in range(groups):
        o = wrap(f + groups - k, groups)
        if k:
            arrive(9, o, scaled_recv.at[o])
        for c in range(2):
            at = pl.multiple_of(o * rows_per + c * half, half)
            logits = logits + dot_rows(
                scaled_recv[o, c * groups : (c + 1) * groups, :], lm[:, pl.ds(at, half)]
            )
    word = iota((1, words), 1) + s * words
    top = jnp.max(jnp.where(word < vocab, logits, -jnp.inf), axis=1, keepdims=True)
    peaks = jnp.where(iota((groups, 128), 1) < 64, top, square_part)
    for o in range(seq_count):
        peak_send[o] = peaks[o * owners : (o + 1) * owners]
    peak_row[s] = peak_send[s]
    across_seq(10, lambda t: peak_send.at[t], lambda me_s: peak_row.at[me_s])
    from_seq(10, lambda o: peak_row.at[o])
    lane = iota((owners, 128), 1)
    peak_recv[f] = jnp.where(lane < 64, jnp.max(peak_row[...], axis=0), peak_row[0])
    across_groups(11, lambda t: peak_recv.at[f], lambda me_f: peak_recv.at[me_f])
    from_groups(11, lambda o: peak_recv.at[o])
    everyone = peak_recv[...]
    best = jnp.max(everyone, axis=0)[:, :1]
    mean_square = jnp.sum(everyone, axis=0)[:, 64:65] / width
    rms_out[...] = jnp.broadcast_to(jnp.sqrt(mean_square), (owners, 128))
    max_out[...] = jnp.broadcast_to(best * lax.rsqrt(mean_square + norm_epsilon), (owners, 128))

    for copy in sent:
        copy.wait_send()

    @pl.when(jnp.logical_not(at_home))
    def _():
        own_key.wait_send()

    for t, copy in own_mix:

        @pl.when(jnp.logical_not(f == t))
        def _(copy=copy):
            copy.wait_send()


def fused(
    text_embeds,
    vision_tokens,
    vision_request,
    image_start,
    lengths,
    attn_gain,
    w_query,
    w_key,
    w_value,
    w_out,
    final_gain,
    lm_head,
):
    groups = lax.axis_size("fsdp")
    seq_count = lax.axis_size("seq")
    seq_len, width = text_embeds.shape
    vtok, piece = vision_tokens.shape
    rows_per, columns = w_query.shape
    words = -(-lm_head.shape[1] // (16 * seq_count)) * 16
    owners = groups // seq_count
    local_heads = columns // HD
    heads = local_heads * seq_count
    capacity = 2 * vtok // groups
    vmem = pl.BlockSpec(memory_space=pltpu.VMEM)
    smem = pl.BlockSpec(memory_space=pltpu.SMEM)
    any_space = pl.BlockSpec(memory_space=pl.ANY)
    phases = 12
    links = max(groups, owners * seq_count)
    rms, best = pl.pallas_call(
        functools.partial(fused_kernel, groups, seq_count, capacity),
        out_shape=[jax.ShapeDtypeStruct((owners, 128), F32)] * 2,
        in_specs=[vmem, smem, smem, vmem, vmem] + [any_space] * 7,
        out_specs=[vmem, vmem],
        scratch_shapes=[
            pltpu.VMEM((seq_len, width), BF16),
            pltpu.VMEM((vtok, piece), BF16),
            pltpu.VMEM((rows_per, columns), BF16),
            pltpu.VMEM((rows_per, columns), BF16),
            pltpu.VMEM((rows_per, columns), BF16),
            pltpu.VMEM((columns, rows_per), BF16),
            pltpu.VMEM((words, width), BF16),
            pltpu.VMEM((seq_len, piece), BF16),
            pltpu.VMEM((heads + 8, piece), F32),
            pltpu.VMEM((groups, local_heads * rows_per // 128, 128), F32),
            pltpu.VMEM((groups, 3, rows_per), F32),
            pltpu.VMEM((groups, 3, rows_per), F32),
            pltpu.VMEM((groups, capacity, piece), BF16),
            pltpu.VMEM((groups, capacity, piece), BF16),
            pltpu.VMEM((2 * groups, columns // 2), BF16),
            pltpu.VMEM((groups, 2 * groups, columns // 2), BF16),
            pltpu.VMEM((groups, local_heads * rows_per // 128, 128), BF16),
            pltpu.VMEM((owners, seq_count, local_heads * rows_per // 128, 128), BF16),
            pltpu.VMEM((seq_count, heads + 8, seq_len), F32),
            pltpu.VMEM((owners, seq_count, local_heads * rows_per // 128, 128), BF16),
            pltpu.VMEM((groups, local_heads * rows_per // 128, 128), BF16),
            pltpu.VMEM((2 * groups, columns // 2), BF16),
            pltpu.VMEM((groups, 2 * groups, columns // 2), BF16),
            pltpu.VMEM((seq_count, groups, rows_per), F32),
            pltpu.VMEM((2 * groups, rows_per // 2), BF16),
            pltpu.VMEM((groups, 2 * groups, rows_per // 2), BF16),
            pltpu.VMEM((seq_count, owners, 128), F32),
            pltpu.VMEM((seq_count, owners, 128), F32),
            pltpu.VMEM((groups, owners, 128), F32),
            pltpu.SemaphoreType.DMA((7,)),
            pltpu.SemaphoreType.DMA((phases, links)),
            pltpu.SemaphoreType.DMA((phases, links)),
        ],
        compiler_params=pltpu.CompilerParams(
            collective_id=0, has_side_effects=True, vmem_limit_bytes=56 * 2**20
        ),
        name="fused",
    )(
        vision_request.reshape(1, vtok),
        image_start,
        lengths,
        attn_gain.reshape(1, width),
        final_gain.reshape(1, width),
        text_embeds,
        vision_tokens,
        w_query,
        w_key,
        w_value,
        w_out,
        lm_head.T,
    )
    return rms[:, 0], best[:, 0]


def fits(mesh):
    groups, seq_count = mesh.shape["fsdp"], mesh.shape["seq"]
    return groups == 8 and groups % seq_count == 0


def solution(mesh):
    return jax.shard_map(
        fused if fits(mesh) else local,
        mesh=mesh,
        in_specs=(
            P("fsdp", None),
            P("fsdp", "seq"),
            P("fsdp", None),
            P("fsdp"),
            P("fsdp"),
            P(),
            P("fsdp", "seq"),
            P("fsdp", "seq"),
            P("fsdp", "seq"),
            P(None, "fsdp"),
            P(),
            P(None, "fsdp"),
        ),
        out_specs=(P("seq"), P("seq")),
        check_vma=False,
    )
```

profile of v0, /device:TPU:0, one launch (start us, length us, event | category | flops | bytes accessed | tf_op | source)
XLA Modules:
  0.0 60.6 jit_solution(2372750352398206440)
XLA Ops:
  1.9 57.3 %fused.1 = (f32[2,128]{1,0:T(2,128)}, f32[2,128]{1,0:T(2,128)}) custom-call(s32[1,128]{1,0:T(1,128)} %bitcast.7, s32[1]{0:T(128)S(6)} %copy.14.start, s32[1]{0:T(128)S(6)} %copy.15.lengths, f32[1,4096]{1,0:T(1,128)} %bitcast.5, f32[1,4096]{1,0:T(1,128)} %bitcast.6, bf16[280,4096]{1,0:T(8,128)(2,1)} %text_hbm.1, bf16[128,1024]{1,0:T(8,128)(2,1)} %vision_hbm.1, ...), custom_call_target="tpu_custom_call" | custom-call | tf_op jit(solution)/shard_map/fused/pallas_call | solution.py:581
  59.2 1.3 %slice_reduce_fusion = (f32[2]{0:T(128)}, f32[2]{0:T(128)}) fusion(f32[2,128]{1,0:T(2,128)} %get-tuple-element.5, f32[2,128]{1,0:T(2,128)} %get-tuple-element.4), kind=kLoop, calls=%fused_computation | loop fusion | bytes 32 | tf_op jit(solution)/shard_map/slice | solution.py:638
where the time goes:
time: 60.9 us; the launch traced here: 60.6 us
  Pallas kernels  57.3 us (94%)
  between operations  1.93 us (3%)
  local copies, waits for them, and re-layouts  1.35 us (2%)
    pallas_call x1, Pallas kernels, fused(): pl.pallas_call(functools.partial(fused_kernel, groups, seq_count, capacit...  57.3 us
    slice x1, local copies, waits for them, and re-layouts, fused(): return (rms[:, 0], best[:, 0])  1.35 us

commit v1 on v0

--- a/solution.py
+++ b/solution.py
@@ -243,8 +243,6 @@
         for j in range(seq_count):
             if k or j:
                 others.append((wrap(f + k, groups), wrap(s + j, seq_count)))
-    for other in others:
-        pl.semaphore_signal(barrier, inc=1, device_id=other, device_id_type=MESH)
 
     def fetch(index, source, target):
         copy = pltpu.make_async_copy(source, target, local_sem.at[index])
@@ -253,6 +251,8 @@
 
     get_text = fetch(0, text_hbm, text)
     get_vision = fetch(1, vision_hbm, vision)
+    for other in others:
+        pl.semaphore_signal(barrier, inc=1, device_id=other, device_id_type=MESH)
     get_wq = fetch(2, wq_hbm, wq)
     get_wk = fetch(3, wk_hbm, wk)
 
@@ -527,7 +527,21 @@
     from_seq(10, lambda o: peak_row.at[o])
     lane = iota((owners, 128), 1)
     peak_recv[f] = jnp.where(lane < 64, jnp.max(peak_row[...], axis=0), peak_row[0])
+    settled = len(sent)
     across_groups(11, lambda t: peak_recv.at[f], lambda me_f: peak_recv.at[me_f])
+    for copy in sent[:settled]:
+        copy.wait_send()
+
+    @pl.when(jnp.logical_not(at_home))
+    def _():
+        own_key.wait_send()
+
+    for t, copy in own_mix:
+
+        @pl.when(jnp.logical_not(f == t))
+        def _(copy=copy):
+            copy.wait_send()
+
     from_groups(11, lambda o: peak_recv.at[o])
     everyone = peak_recv[...]
     best = jnp.max(everyone, axis=0)[:, :1]
@@ -535,18 +549,8 @@
     rms_out[...] = jnp.broadcast_to(jnp.sqrt(mean_square), (owners, 128))
     max_out[...] = jnp.broadcast_to(best * lax.rsqrt(mean_square + norm_epsilon), (owners, 128))
 
-    for copy in sent:
+    for copy in sent[settled:]:
         copy.wait_send()
-
-    @pl.when(jnp.logical_not(at_home))
-    def _():
-        own_key.wait_send()
-
-    for t, copy in own_mix:
-
-        @pl.when(jnp.logical_not(f == t))
-        def _(copy=copy):
-            copy.wait_send()
 
 
 def fused(

time: 60.9 us -> 60.8 us (level)
  no operation moved by 1% of the time
where the time goes in v1:
time: 60.8 us; the launch traced here: 60.5 us
  Pallas kernels  57.2 us (94%)
  between operations  1.93 us (3%)
  local copies, waits for them, and re-layouts  1.35 us (2%)
    pallas_call x1, Pallas kernels, fused(): pl.pallas_call(functools.partial(fused_kernel, groups, seq_count, capacit...  57.2 us
    slice x1, local copies, waits for them, and re-layouts, fused(): return (rms[:, 0], best[:, 0])  1.35 us

profile of v1, /device:TPU:0, one launch (start us, length us, event | category | flops | bytes accessed | tf_op | source)
XLA Modules:
  0.0 60.5 jit_solution(7049119497681378604)
XLA Ops:
  1.9 57.2 %fused.1 = (f32[2,128]{1,0:T(2,128)}, f32[2,128]{1,0:T(2,128)}) custom-call(s32[1,128]{1,0:T(1,128)} %bitcast.7, s32[1]{0:T(128)S(6)} %copy.14.start, s32[1]{0:T(128)S(6)} %copy.15.lengths, f32[1,4096]{1,0:T(1,128)} %bitcast.5, f32[1,4096]{1,0:T(1,128)} %bitcast.6, bf16[280,4096]{1,0:T(8,128)(2,1)} %text_hbm.1, bf16[128,1024]{1,0:T(8,128)(2,1)} %vision_hbm.1, ...), custom_call_target="tpu_custom_call" | custom-call | tf_op jit(solution)/shard_map/fused/pallas_call | solution.py:585
  59.1 1.3 %slice_reduce_fusion = (f32[2]{0:T(128)}, f32[2]{0:T(128)}) fusion(f32[2,128]{1,0:T(2,128)} %get-tuple-element.5, f32[2,128]{1,0:T(2,128)} %get-tuple-element.4), kind=kLoop, calls=%fused_computation | loop fusion | bytes 32 | tf_op jit(solution)/shard_map/slice | solution.py:642
